TPU v7x, 32 devices: a whole 2x2x4 slice. The times are simulated.
32 devices in a mesh: dp: 4 (over y, core), head: 8 (over z, x).
Axes of the slice: x: 2, y: 2, z: 4, core: 2. Of those that a mesh axis runs over, the one named last changes fastest.
Arguments:
- latent: bfloat16 [4096, 1536], P('dp', 'head'), may hold values from -6 to 6
- weight: bfloat16 [1536, 24576], P(None, 'head'), may hold values from -0.15625 to 0.15625
- query_grad: bfloat16 [4096, 24576], P('dp', 'head'), may hold values from -6 to 6
- master: float32 [1536, 24576], P('dp', 'head'), may hold values from -6 to 6
- first_moment: float32 [1536, 24576], P('dp', 'head'), may hold values from -6 to 6
- second_moment: float32 [1536, 24576], P('dp', 'head'), may hold values from 100 to 10000
Outputs:
- queries: bfloat16 [4096, 24576], P('dp', 'head')
- latent_grad: bfloat16 [4096, 1536], P('dp', 'head')
- new_master: float32 [1536, 24576], P('dp', 'head')
- new_first: float32 [1536, 24576], P('dp', 'head')
- new_second: float32 [1536, 24576], P('dp', 'head')
All inputs are finite; a program needn't handle non-finite values.
Results may differ from a plain program's by a relative error of at most 0.014.
Values may be sent and summed in bfloat16 or wider, within the bound.
A program may use at most 128 MiB of HBM per device.

v0:
```python
import jax
import jax.numpy as jnp
from jax import lax
from jax.sharding import PartitionSpec as P

STEP = 10


def on_device(latent, weight, query_grad, master, first_moment, second_moment):
    lat_full = lax.all_gather(latent, "head", axis=1, tiled=True)
    queries = jnp.dot(lat_full, weight, preferred_element_type=jnp.float32).astype(jnp.bfloat16)
    partial_lat = lax.dot_general(
        query_grad, weight, (((1,), (1,)), ((), ())), preferred_element_type=jnp.float32
    )
    latent_grad = lax.psum_scatter(
        partial_lat.astype(jnp.bfloat16), "head", scatter_dimension=1, tiled=True
    )
    partial_w = lax.dot_general(
        lat_full, query_grad, (((0,), (0,)), ((), ())), preferred_element_type=jnp.float32
    )
    grad = lax.psum_scatter(
        partial_w.astype(jnp.bfloat16), "dp", scatter_dimension=0, tiled=True
    ).astype(jnp.float32)
    new_first = 0.9 * first_moment + 0.1 * grad
    new_second = 0.95 * second_moment + 0.05 * grad * grad
    first_hat = new_first / (1.0 - 0.9**STEP)
    second_hat = new_second / (1.0 - 0.95**STEP)
    new_master = master - 0.01 * (first_hat / (jnp.sqrt(second_hat) + 1e-08) + 0.1 * master)
    return (queries, latent_grad, new_master, new_first, new_second)


def solution(mesh):
    return jax.shard_map(
        on_device,
        mesh=mesh,
        in_specs=(
            P("dp", "head"),
            P(None, "head"),
            P("dp", "head"),
            P("dp", "head"),
            P("dp", "head"),
            P("dp", "head"),
        ),
        out_specs=(
            P("dp", "head"),
            P("dp", "head"),
            P("dp", "head"),
            P("dp", "head"),
            P("dp", "head"),
        ),
        check_vma=False,
    )
```

profile of v0, /device:TPU:12, one launch (start us, length us, event | category | flops | bytes accessed | tf_op | source)
XLA Modules:
  0.0 249.0 jit_solution(973708358567710531)
XLA Ops:
  7.2 0.0 all-gather.2.cloned.1.call-start
  7.2 0.7 all-gather.2.cloned.1.call-update
  7.9 0.0 reduce-scatter.5.cloned.1.call-start
  7.9 63.8 %all-gather.2.cloned.1.call-done = bf16[1024,1536]{0,1:T(8,128)(2,1)} async-done(((bf16[1024,192]{0,1:T(8,128)(2,1)}), bf16[1024,1536]{0,1:T(8,128)(2,1)}) %all-gather.2.cloned.1.call-update) | async-done | bytes 3145744 | tf_op jit(solution)/shard_map/all_gather | solution.py:10
  71.7 15.3 %convolution_convert_fusion = bf16[1536,3072]{1,0:T(8,128)(2,1)} fusion(bf16[1024,1536]{0,1:T(8,128)(2,1)} %all-gather.2.cloned.1.call-done, bf16[1024,3072]{1,0:T(8,128)(2,1)} %param.8), kind=kOutput, calls=%fused_computation | convolution fusion | flops 9668395008 | bytes 18874368 | tf_op jit(solution)/shard_map/dot_general | solution.py:18
  87.0 0.0 reduce-scatter.5.cloned.1.call-update
  87.1 0.0 copy-start
  87.1 0.2 reduce-scatter.3.cloned.1.call-start
  87.3 15.7 %convolution_convert_fusion.2 = bf16[1024,1536]{0,1:T(8,128)(2,1)} fusion(bf16[1024,3072]{1,0:T(8,128)(2,1)} %param.8, bf16[1536,3072]{1,0:T(8,128)(2,1)} %param.7), kind=kOutput, calls=%fused_computation.7 | convolution fusion | flops 9665249280 | bytes 18874368 | tf_op jit(solution)/shard_map/dot_general | solution.py:12
  103.0 0.0 reduce-scatter.3.cloned.1.call-update
  103.0 0.0 copy-done
  103.0 14.3 %convolution_convert_fusion.1 = bf16[1024,3072]{1,0:T(8,128)(2,1)} fusion(bf16[1024,1536]{0,1:T(8,128)(2,1)S(1)} %copy-done, bf16[1536,3072]{1,0:T(8,128)(2,1)} %param.7), kind=kOutput, calls=%fused_computation.3 | convolution fusion | flops 9666822144 | bytes 18874368 | tf_op jit(solution)/shard_map/dot_general | solution.py:11
  117.4 46.1 %reduce-scatter.5.cloned.1.call-done = bf16[384,3072]{1,0:T(8,128)(2,1)} async-done(((bf16[1536,3072]{1,0:T(8,128)(2,1)}), bf16[384,3072]{1,0:T(8,128)(2,1)}) %reduce-scatter.5.cloned.1.call-update) | async-done | bytes 2359312 | tf_op jit(solution)/shard_map/reduce_scatter | solution.py:21
  163.4 11.2 %multiply_subtract_fusion = (f32[384,3072]{1,0:T(8,128)}, f32[384,3072]{1,0:T(8,128)}, f32[384,3072]{1,0:T(8,128)}) fusion(f32[384,3072]{1,0:T(8,128)} %param.9, bf16[384,3072]{1,0:T(8,128)(2,1)} %reduce-scatter.5.cloned.1.call-done, f32[384,3072]{1,0:T(8,128)} %param.10, f32[384,3072]{1,0:T(8,128)} %param.11), kind=kLoop, calls=%fused_computation.6 | loop fusion | flops 18874368 | bytes 30670848 | tf_op jit(solution)/shard_map/sub | solution.py:28
  174.6 67.8 %reduce-scatter.3.cloned.1.call-done = bf16[1024,192]{0,1:T(8,128)(2,1)} async-done(((bf16[1024,1536]{0,1:T(8,128)(2,1)}), bf16[1024,192]{0,1:T(8,128)(2,1)}) %reduce-scatter.3.cloned.1.call-update) | async-done | bytes 393232 | tf_op jit(solution)/shard_map/reduce_scatter | solution.py:15
Async XLA Ops:
  7.2 64.6 %all-gather.2.cloned.1.call-start = ((), (), s32[]{:S(2)}) async-start(), calls=%async_computation.2 | async-start | bytes 3538944 | tf_op jit(solution)/shard_map/all_gather | solution.py:10
  7.9 155.5 %reduce-scatter.5.cloned.1.call-start = ((), (), s32[]{:S(2)}) async-start(), calls=%async_computation.4 | async-start | bytes 11796480 | tf_op jit(solution)/shard_map/reduce_scatter | solution.py:21
  87.1 16.0 %copy-start = (bf16[1024,1536]{0,1:T(8,128)(2,1)S(1)}, bf16[1024,1536]{0,1:T(8,128)(2,1)}, u32[]{:S(2)}) copy-start(bf16[1024,1536]{0,1:T(8,128)(2,1)} %all-gather.2.cloned.1.call-done) | copy-start | bytes 9437188
  87.1 155.4 %reduce-scatter.3.cloned.1.call-start = ((), (), s32[]{:S(2)}) async-start(), calls=%async_computation.3 | async-start | bytes 3538944 | tf_op jit(solution)/shard_map/reduce_scatter | solution.py:15
Sparse Core Ops, SparseCore 0:
  10.2 61.5 all-gather.1
  87.2 76.2 reduce-scatter.4
  167.6 74.8 reduce-scatter.2
where the time goes:
time: 251 us; the launch traced here: 249 us
  waiting for transfers between devices  178 us (71%)
  matrix products  45.3 us (18%)
  between operations  13.8 us (5%)
  other arithmetic  11.2 us (4%)
    reduce_scatter x1, waiting for transfers between devices, on_device(): lax.psum_scatter(partial_lat.astype(jnp.bfloat16), 'head', scatter_dimens...  67.8 us
    all_gather x1, waiting for transfers between devices, on_device(): lat_full = lax.all_gather(latent, 'head', axis=1, tiled=True)  63.8 us
    reduce_scatter x1, waiting for transfers between devices, on_device(): lax.psum_scatter(partial_w.astype(jnp.bfloat16), 'dp', scatter_dimension=...  46.1 us
    dot_general x1, matrix products, on_device(): lax.dot_general(query_grad, weight, (((1,), (1,)), ((), ())), preferred_e...  15.7 us
    dot_general x1, matrix products, on_device(): lax.dot_general(lat_full, query_grad, (((0,), (0,)), ((), ())), preferred...  15.3 us
    dot_general x1, matrix products, on_device(): jnp.dot(lat_full, weight, preferred_element_type=jnp.float32)  14.3 us
    sub x1, other arithmetic, on_device(): master - 0.01 * (first_hat / (jnp.sqrt(second_hat) + 1e-08) + 0.1 * master)  11.2 us
  transfers between devices with their start and end apart: 3, of which 3 were waited for; matrix products, arithmetic and copies ran while one was open for 17% of the time, Pallas kernels for 0%

commit v1 on v0

v1 whole, which is shorter than its diff:
```python
import functools
import math

import jax
import jax.numpy as jnp
from jax import lax
from jax.experimental import pallas as pl
from jax.experimental.pallas import tpu as pltpu
from jax.sharding import PartitionSpec as P

STEP = 10
CORES = 2
MESH = pl.DeviceIdType.MESH


def flip(a, k):
    out = a
    b = 1
    while b <= k:
        if k & b:
            out = out + b * (1 - 2 * lax.rem(lax.div(a, b), 2))
        b *= 2
    return out


def kernel(sizes, lat_ref, w_hbm, qg_hbm, q_hbm, lg_ref, grad_ref,
           w, qg, lat, part, sib, ybuf, plat, xbuf, zbuf, lhs, qs,
           w_sem, qg_sem, own_sem, q_sem,
           az_s, az_r, ax_s, ax_r, lx_s, lx_r, lz_s, lz_r, ws_s, ws_r, wy_s, wy_r):
    Z, X, Y, R, NC, C, NT, T, NQ, TQ = sizes
    dp = lax.axis_index("dp")
    head = lax.axis_index("head")
    y, core = lax.div(dp, CORES), lax.rem(dp, CORES)
    z, x = lax.div(head, X), lax.rem(head, X)
    D = w_hbm.shape[0]
    rows = part.shape[2]
    B = lat.shape[2]
    f32 = jnp.float32

    def load_qg():
        return pltpu.make_async_copy(qg_hbm, qg, qg_sem)

    def load_w(kz):
        zz = flip(z, kz)
        return pltpu.make_async_copy(w_hbm.at[pl.ds(pl.multiple_of(zz * (X * B), X * B), X * B), :], w.at[zz], w_sem.at[kz])

    def own():
        return pltpu.make_async_copy(lat_ref, lat.at[z, x], own_sem)

    bits = [1 << i for i in range(int(math.log2(Z)))][::-1]
    order = [sum(((k >> i) & 1) << (len(bits) - 1 - i) for i in range(len(bits))) for k in range(Z)]
    far = order[1:][::-1][::-1]
    load_qg().start()
    for kz in order:
        load_w(kz).start()
    own().start()

    barrier = pltpu.get_barrier_semaphore()
    peers = [(y * CORES + 1 - core, head)]
    peers += [(flip(y, k) * CORES + core, head) for k in range(1, Y)]
    peers += [(dp, flip(z, k) * X + x) for k in range(1, Z)]
    peers += [(dp, z * X + flip(x, k)) for k in range(1, X)]
    for peer in peers:
        pl.semaphore_signal(barrier, inc=1, device_id=peer, device_id_type=MESH)
    pl.semaphore_wait(barrier, len(peers))

    def send_az(kz, bit):
        zz = flip(z, kz)
        return pltpu.make_async_remote_copy(
            src_ref=lat.at[zz, x], dst_ref=lat.at[zz, x],
            send_sem=az_s.at[kz ^ bit], recv_sem=az_r.at[kz ^ bit],
            device_id=(dp, flip(z, bit) * X + x), device_id_type=MESH)

    def recv_az(kz):
        zz = flip(z, kz)
        return pltpu.make_async_remote_copy(
            src_ref=lat.at[zz, x], dst_ref=lat.at[zz, x],
            send_sem=az_s.at[kz], recv_sem=az_r.at[kz],
            device_id=(dp, flip(z, kz & -kz) * X + x), device_id_type=MESH)

    def send_ax(kz, kx):
        zz = flip(z, kz)
        return pltpu.make_async_remote_copy(
            src_ref=lat.at[zz, x], dst_ref=lat.at[zz, x],
            send_sem=ax_s.at[kz, kx], recv_sem=ax_r.at[kz, kx],
            device_id=(dp, z * X + flip(x, kx)), device_id_type=MESH)

    def recv_ax(kz, kx):
        zz = flip(z, kz)
        xx = flip(x, kx)
        return pltpu.make_async_remote_copy(
            src_ref=lat.at[zz, xx], dst_ref=lat.at[zz, xx],
            send_sem=ax_s.at[kz, kx], recv_sem=ax_r.at[kz, kx],
            device_id=(dp, z * X + xx), device_id_type=MESH)

    def low(kz):
        return [b for b in bits if kz == 0 or b < (kz & -kz)]

    def forward(kz):
        if kz:
            recv_az(kz).wait_recv()
        for bit in low(kz):
            send_az(kz, bit).start()
        for kx in range(1, X):
            send_ax(kz, kx).start()

    def send_lx(kz, kx):
        zz, xx = flip(z, kz), flip(x, kx)
        return pltpu.make_async_remote_copy(
            src_ref=plat.at[zz, xx], dst_ref=xbuf.at[kx - 1, kz],
            send_sem=lx_s.at[kz, kx], recv_sem=lx_r.at[kz, kx],
            device_id=(dp, z * X + xx), device_id_type=MESH)

    def send_lz(kz):
        zz = flip(z, kz)
        return pltpu.make_async_remote_copy(
            src_ref=plat.at[zz, x], dst_ref=zbuf.at[kz - 1],
            send_sem=lz_s.at[kz], recv_sem=lz_r.at[kz],
            device_id=(dp, zz * X + x), device_id_type=MESH)

    def lat_share(kz):
        zz = flip(z, kz)

        @pl.loop(0, NT)
        def _(t):
            cols = pl.ds(pl.multiple_of(t * T, T), T)
            res = lax.dot_general(w[zz], qg[cols, :], (((1,), (1,)), ((), ())), preferred_element_type=f32)
            plat[zz, :, :, cols] = res.astype(jnp.bfloat16).reshape(X, B, T)

        for kx in range(1, X):
            send_lx(kz, kx).start()

    def lat_sum_x(kz):
        zz = flip(z, kz)
        for kx in range(1, X):
            send_lx(kz, kx).wait_recv()
        total = plat[zz, x].astype(f32)
        for kx in range(1, X):
            total = total + xbuf[kx - 1, kz].astype(f32)
        if kz:
            plat[zz, x] = total.astype(jnp.bfloat16)
            send_lz(kz).start()
        else:
            for k in range(1, Z):
                send_lz(k).wait_recv()
                total = total + zbuf[k - 1].astype(f32)
            lg_ref[...] = total.astype(jnp.bfloat16)

    def send_ws(g, c):
        p = lax.div(g, CORES)
        return pltpu.make_async_remote_copy(
            src_ref=part.at[g, c], dst_ref=sib.at[p, c],
            send_sem=ws_s.at[p, c], recv_sem=ws_r.at[p, c],
            device_id=(y * CORES + 1 - core, head), device_id_type=MESH)

    def send_wy(p, c):
        slot = lax.rem(y - p + Y, Y) - 1
        return pltpu.make_async_remote_copy(
            src_ref=part.at[p * CORES + core, c], dst_ref=ybuf.at[slot, c],
            send_sem=wy_s.at[slot, c], recv_sem=wy_r.at[slot, c],
            device_id=(p * CORES + core, head), device_id_type=MESH)

    def w_share(kz):
        zz = flip(z, kz)
        for kx in range(1, X):
            recv_ax(kz, kx).wait_recv()
        for r in range(R):
            g = zz * R + r

            @pl.loop(0, NC)
            def _(c):
                cols = pl.ds(pl.multiple_of(c * C, C), C)
                left = lat[zz].reshape(X * B, -1)[r * rows:(r + 1) * rows, :]
                res = jnp.dot(left, qg[:, cols], preferred_element_type=f32)
                part[g, c] = res.astype(jnp.bfloat16)

                @pl.when(lax.rem(g, CORES) != core)
                def _():
                    send_ws(g, c).start()

    def w_sum(kz):
        zz = flip(z, kz)
        for r in range(R):
            g = zz * R + r
            p = lax.div(g, CORES)

            @pl.when((lax.rem(g, CORES) == core) & (p != y))
            def _():
                @pl.loop(0, NC)
                def _(c):
                    send_ws(g, c).wait_recv()
                    total = part[g, c].astype(f32) + sib[p, c].astype(f32)
                    part[g, c] = total.astype(jnp.bfloat16)
                    send_wy(p, c).start()

    def q_out(t, c):
        return pltpu.make_async_copy(
            qs.at[t, c],
            q_hbm.at[pl.ds(pl.multiple_of(t * TQ, TQ), TQ), pl.ds(pl.multiple_of(c * C, C), C)],
            q_sem.at[t, c])

    def queries():
        @pl.loop(0, NQ)
        def _(t):
            toks = pl.ds(pl.multiple_of(t * TQ, TQ), TQ)
            lhs[...] = lat[:, :, :, toks].reshape(D, TQ).T

            @pl.loop(0, NC)
            def _(c):
                cols = pl.ds(pl.multiple_of(c * C, C), C)
                res = jnp.dot(lhs[...], w[:, :, cols].reshape(D, C), preferred_element_type=f32)
                qs[t, c] = res.astype(jnp.bfloat16)
                q_out(t, c).start()

    own().wait()
    forward(0)
    load_qg().wait()
    seq = order[1:] + [0]
    for kz in order:
        load_w(kz).wait()
    lat_share(seq[0])
    w_share(0)
    w_sum(0)
    done = {seq[0]}
    arrive = sorted(range(1, Z), key=lambda k: (bin(k).count("1"), k))
    for kz in arrive:
        forward(kz)
        nxt = [k for k in seq if k not in done]
        if nxt:
            lat_share(nxt[0])
            done.add(nxt[0])
    for kz in seq:
        if kz not in done:
            lat_share(kz)
    for kz in order[1:]:
        w_share(kz)
        w_sum(kz)
    for kz in order[1:]:
        lat_sum_x(kz)
    queries()
    lat_sum_x(0)

    @pl.loop(0, NC)
    def _(c):
        mine = y * CORES + core
        send_ws(mine, c).wait_recv()
        total = part[mine, c].astype(f32) + sib[y, c].astype(f32)
        for k in range(1, Y):
            p = lax.rem(y + k, Y)
            other = pltpu.make_async_remote_copy(
                src_ref=part.at[p * CORES + core, c], dst_ref=ybuf.at[k - 1, c],
                send_sem=wy_s.at[k - 1, c], recv_sem=wy_r.at[k - 1, c],
                device_id=(p * CORES + core, head), device_id_type=MESH)
            other.wait_recv()
            total = total + ybuf[k - 1, c].astype(f32)
        grad_ref[:, pl.ds(pl.multiple_of(c * C, C), C)] = total

    for kz in range(Z):
        for bit in low(kz):
            send_az(kz, bit).wait_send()
        for kx in range(1, X):
            send_ax(kz, kx).wait_send()
            send_lx(kz, kx).wait_send()
        if kz:
            send_lz(kz).wait_send()

    @pl.loop(0, NC)
    def _(c):
        for p in range(Y):
            send_ws(p * CORES + 1 - core, c).wait_send()
        for k in range(1, Y):
            send_wy(lax.rem(y - k + Y, Y), c).wait_send()
        for t in range(NQ):
            q_out(t, c).wait()


def on_device(n_dp, n_head, latent, weight, query_grad, master, first_moment, second_moment):
    T_all, B = latent.shape
    D, width = weight.shape
    X = 1 << (int(math.log2(n_head)) // 2)
    Z = n_head // X
    Y = n_dp // CORES
    R = n_dp // Z
    rows = D // n_dp
    C = 1024 if width % 1024 == 0 else 512
    NC = width // C
    T = min(256, T_all)
    NT = T_all // T
    TQ = min(512, T_all)
    NQ = T_all // TQ
    bf = jnp.bfloat16
    sem = pltpu.SemaphoreType.DMA
    vmem = pl.BlockSpec(memory_space=pltpu.VMEM)
    hbm = pl.BlockSpec(memory_space=pl.ANY)
    queries, lgt, grad = pl.pallas_call(
        functools.partial(kernel, (Z, X, Y, R, NC, C, NT, T, NQ, TQ)),
        out_shape=(
            jax.ShapeDtypeStruct((T_all, width), bf),
            jax.ShapeDtypeStruct((B, T_all), bf),
            jax.ShapeDtypeStruct((rows, width), jnp.float32),
        ),
        in_specs=[vmem, hbm, hbm],
        out_specs=(hbm, vmem, vmem),
        scratch_shapes=[
            pltpu.VMEM((Z, X * B, width), bf),
            pltpu.VMEM((T_all, width), bf),
            pltpu.VMEM((Z, X, B, T_all), bf),
            pltpu.VMEM((n_dp, NC, rows, C), bf),
            pltpu.VMEM((Y, NC, rows, C), bf),
            pltpu.VMEM((max(Y - 1, 1), NC, rows, C), bf),
            pltpu.VMEM((Z, X, B, T_all), bf),
            pltpu.VMEM((X - 1, Z, B, T_all), bf),
            pltpu.VMEM((Z - 1, B, T_all), bf),
            pltpu.VMEM((TQ, D), bf),
            pltpu.VMEM((NQ, NC, TQ, C), bf),
            sem((Z,)), sem, sem, sem((NQ, NC)),
            sem((Z,)), sem((Z,)), sem((Z, X)), sem((Z, X)),
            sem((Z, X)), sem((Z, X)), sem((Z,)), sem((Z,)),
            sem((Y, NC)), sem((Y, NC)), sem((max(Y - 1, 1), NC)), sem((max(Y - 1, 1), NC)),
        ],
        compiler_params=pltpu.CompilerParams(
            collective_id=0, has_side_effects=True, vmem_limit_bytes=60 * 1024 * 1024
        ),
        cost_estimate=pl.CostEstimate(
            flops=6 * T_all * D * width, bytes_accessed=4 * (D + T_all) * width, transcendentals=0
        ),
    )(latent.T, weight, query_grad)
    latent_grad = lgt.T
    new_first = 0.9 * first_moment + 0.1 * grad
    new_second = 0.95 * second_moment + 0.05 * grad * grad
    first_hat = new_first / (1.0 - 0.9**STEP)
    second_hat = new_second / (1.0 - 0.95**STEP)
    new_master = master - 0.01 * (first_hat / (jnp.sqrt(second_hat) + 1e-08) + 0.1 * master)
    return (queries, latent_grad, new_master, new_first, new_second)


def solution(mesh):
    return jax.shard_map(
        functools.partial(on_device, mesh.shape["dp"], mesh.shape["head"]),
        mesh=mesh,
        in_specs=(P("dp", "head"), P(None, "head")) + (P("dp", "head"),) * 4,
        out_specs=(P("dp", "head"),) * 5,
        check_vma=False,
    )
```

time: 251 us -> 126 us (0.50)
  waiting for transfers between devices: 178 us -> 0 us
  Pallas kernels: 0 us -> 110 us
  matrix products: 45.3 us -> 0 us
  between operations: 13.8 us -> 0.65 us
  local copies, waits for them, and re-layouts: 0.01 us -> 3.46 us
    reduce_scatter x2 -> x0, waiting for transfers between devices: 114 us -> none  [the longest x1 67.8 us: on_device(): lax.psum_scatter(partial_lat.astype(jnp.bfloat16), 'head', scatter_dimens...]
    pallas_call x0 -> x1, Pallas kernels: none -> 110 us  [on_device(): pl.pallas_call(functools.partial(kernel, (Z, X, Y, R, NC, C, NT, T, NQ, T...]
    all_gather x1 -> x0, waiting for transfers between devices: 63.8 us -> none  [on_device(): lat_full = lax.all_gather(latent, 'head', axis=1, tiled=True)]
    dot_general x3 -> x0, matrix products: 45.3 us -> none  [the longest x1 15.7 us: on_device(): lax.dot_general(query_grad, weight, (((1,), (1,)), ((), ())), preferred_e...]
    unnamed x2 -> x6, local copies, waits for them, and re-layouts: 0.01 us -> 3.46 us
  transfers between devices with their start and end apart: 3 -> 0, of which waited for: 3 -> 0; matrix products, arithmetic and copies ran while one was open for 17% -> 0% of each run, Pallas kernels for 0% -> 0%
where the time goes in v1:
time: 126 us
  Pallas kernels  110 us (87%)
  other arithmetic  12.6 us (10%)
  local copies, waits for them, and re-layouts  3.46 us (3%)
    pallas_call x1, Pallas kernels, on_device(): pl.pallas_call(functools.partial(kernel, (Z, X, Y, R, NC, C, NT, T, NQ, T...  110 us
    sub x1, other arithmetic, on_device(): master - 0.01 * (first_hat / (jnp.sqrt(second_hat) + 1e-08) + 0.1 * master)  12.6 us
    unnamed x6, local copies, waits for them, and re-layouts  3.46 us

profile of v1, /device:TPU:12, one launch (start us, length us, event | category | flops | bytes accessed | tf_op | source)
XLA Modules:
  0.0 126.3 jit_solution(3584704988600000290)
XLA Ops:
  0.6 109.6 %shard_map.101 = (bf16[1024,3072]{1,0:T(8,128)(2,1)}, bf16[192,1024]{1,0:T(8,128)(2,1)}, f32[384,3072]{1,0:T(8,128)}) custom-call(bf16[192,1024]{1,0:T(8,128)(2,1)} %bitcast.3, bf16[1536,3072]{1,0:T(8,128)(2,1)} %w_hbm.1, bf16[1024,3072]{1,0:T(8,128)(2,1)} %qg_hbm.1), custom_call_target="tpu_custom_call" | custom-call | flops 28991029248 | bytes 31457280 | tf_op jit(solution)/shard_map/pallas_call | solution.py:295
  110.2 0.0 copy-start
  110.2 12.6 %multiply_subtract_fusion = (f32[384,3072]{1,0:T(8,128)}, f32[384,3072]{1,0:T(8,128)}, f32[384,3072]{1,0:T(8,128)}) fusion(f32[384,3072]{1,0:T(8,128)} %param.9, f32[384,3072]{1,0:T(8,128)} %get-tuple-element.10, f32[384,3072]{1,0:T(8,128)} %param.10, f32[384,3072]{1,0:T(8,128)} %param.11), kind=kLoop, calls=%fused_computation.2 | loop fusion | flops 17694720 | bytes 33030144 | tf_op jit(solution)/shard_map/sub | solution.py:333
  122.9 0.0 copy-done
  122.9 0.0 copy-start.1
  122.9 2.7 %copy.13 = bf16[1024,3072]{1,0:T(8,128)(2,1)} copy(bf16[1024,3072]{1,0:T(8,128)(2,1)S(1)} %copy-done) | data formatting | bytes 12582912
  125.6 0.0 copy-done.1
  125.6 0.7 copy.14
Async XLA Ops:
  110.2 12.6 %copy-start = (bf16[1024,3072]{1,0:T(8,128)(2,1)S(1)}, bf16[1024,3072]{1,0:T(8,128)(2,1)}, u32[]{:S(2)}) copy-start(bf16[1024,3072]{1,0:T(8,128)(2,1)} %get-tuple-element.19) | copy-start | bytes 18874372
  122.9 2.7 %copy-start.1 = (bf16[192,1024]{1,0:T(8,128)(2,1)S(1)}, bf16[192,1024]{1,0:T(8,128)(2,1)}, u32[]{:S(2)}) copy-start(bf16[192,1024]{1,0:T(8,128)(2,1)} %get-tuple-element.9) | copy-start | bytes 1179652

commit v2 on v1

--- a/solution.py
+++ b/solution.py
@@ -27,13 +27,12 @@
            w, qg, lat, part, sib, ybuf, plat, xbuf, zbuf, lhs, qs,
            w_sem, qg_sem, own_sem, q_sem,
            az_s, az_r, ax_s, ax_r, lx_s, lx_r, lz_s, lz_r, ws_s, ws_r, wy_s, wy_r):
-    Z, X, Y, R, NC, C, NT, T, NQ, TQ = sizes
+    Z, X, Y, Q, NC, C, NT, T, NQ, TQ = sizes
     dp = lax.axis_index("dp")
     head = lax.axis_index("head")
     y, core = lax.div(dp, CORES), lax.rem(dp, CORES)
     z, x = lax.div(head, X), lax.rem(head, X)
     D = w_hbm.shape[0]
-    rows = part.shape[2]
     B = lat.shape[2]
     f32 = jnp.float32
 
@@ -49,7 +48,6 @@
 
     bits = [1 << i for i in range(int(math.log2(Z)))][::-1]
     order = [sum(((k >> i) & 1) << (len(bits) - 1 - i) for i in range(len(bits))) for k in range(Z)]
-    far = order[1:][::-1][::-1]
     load_qg().start()
     for kz in order:
         load_w(kz).start()
@@ -146,52 +144,50 @@
                 total = total + zbuf[k - 1].astype(f32)
             lg_ref[...] = total.astype(jnp.bfloat16)
 
-    def send_ws(g, c):
+    def send_ws(h, c):
+        p, j = lax.div(h, Q * CORES), lax.rem(h, Q)
+        return pltpu.make_async_remote_copy(
+            src_ref=part.at[h, c], dst_ref=sib.at[p, j, c],
+            send_sem=ws_s.at[p, j, c], recv_sem=ws_r.at[p, j, c],
+            device_id=(y * CORES + 1 - core, head), device_id_type=MESH)
+
+    def copy_wy(h, p, slot, c):
+        j = lax.rem(h, Q)
+        return pltpu.make_async_remote_copy(
+            src_ref=part.at[h, c], dst_ref=ybuf.at[slot, j, c],
+            send_sem=wy_s.at[slot, j, c], recv_sem=wy_r.at[slot, j, c],
+            device_id=(p * CORES + core, head), device_id_type=MESH)
+
+    def w_share(kz, kx):
+        zz, xx = flip(z, kz), flip(x, kx)
+        if kx:
+            recv_ax(kz, kx).wait_recv()
+        h = zz * X + xx
+        g = lax.div(h, Q)
+
+        @pl.loop(0, NC)
+        def _(c):
+            cols = pl.ds(pl.multiple_of(c * C, C), C)
+            res = jnp.dot(lat[zz, xx], qg[:, cols], preferred_element_type=f32)
+            part[h, c] = res.astype(jnp.bfloat16)
+
+            @pl.when(lax.rem(g, CORES) != core)
+            def _():
+                send_ws(h, c).start()
+
+    def w_sum(kz, kx):
+        h = flip(z, kz) * X + flip(x, kx)
+        g = lax.div(h, Q)
         p = lax.div(g, CORES)
-        return pltpu.make_async_remote_copy(
-            src_ref=part.at[g, c], dst_ref=sib.at[p, c],
-            send_sem=ws_s.at[p, c], recv_sem=ws_r.at[p, c],
-            device_id=(y * CORES + 1 - core, head), device_id_type=MESH)
-
-    def send_wy(p, c):
-        slot = lax.rem(y - p + Y, Y) - 1
-        return pltpu.make_async_remote_copy(
-            src_ref=part.at[p * CORES + core, c], dst_ref=ybuf.at[slot, c],
-            send_sem=wy_s.at[slot, c], recv_sem=wy_r.at[slot, c],
-            device_id=(p * CORES + core, head), device_id_type=MESH)
-
-    def w_share(kz):
-        zz = flip(z, kz)
-        for kx in range(1, X):
-            recv_ax(kz, kx).wait_recv()
-        for r in range(R):
-            g = zz * R + r
-
+
+        @pl.when((lax.rem(g, CORES) == core) & (p != y))
+        def _():
             @pl.loop(0, NC)
             def _(c):
-                cols = pl.ds(pl.multiple_of(c * C, C), C)
-                left = lat[zz].reshape(X * B, -1)[r * rows:(r + 1) * rows, :]
-                res = jnp.dot(left, qg[:, cols], preferred_element_type=f32)
-                part[g, c] = res.astype(jnp.bfloat16)
-
-                @pl.when(lax.rem(g, CORES) != core)
-                def _():
-                    send_ws(g, c).start()
-
-    def w_sum(kz):
-        zz = flip(z, kz)
-        for r in range(R):
-            g = zz * R + r
-            p = lax.div(g, CORES)
-
-            @pl.when((lax.rem(g, CORES) == core) & (p != y))
-            def _():
-                @pl.loop(0, NC)
-                def _(c):
-                    send_ws(g, c).wait_recv()
-                    total = part[g, c].astype(f32) + sib[p, c].astype(f32)
-                    part[g, c] = total.astype(jnp.bfloat16)
-                    send_wy(p, c).start()
+                send_ws(h, c).wait_recv()
+                total = part[h, c].astype(f32) + sib[p, lax.rem(h, Q), c].astype(f32)
+                part[h, c] = total.astype(jnp.bfloat16)
+                copy_wy(h, p, lax.rem(y - p + Y, Y) - 1, c).start()
 
     def q_out(t, c):
         return pltpu.make_async_copy(
@@ -215,45 +211,60 @@
     own().wait()
     forward(0)
     load_qg().wait()
-    seq = order[1:] + [0]
-    for kz in order:
+    xs = list(range(1, X))
+    tail = order[1:]
+    turns = iter(tail + [0])
+
+    def lat_next():
+        kz = next(turns, None)
+        if kz is not None:
+            lat_share(kz)
+
+    w_share(0, 0)
+    for kz in range(Z):
         load_w(kz).wait()
-    lat_share(seq[0])
-    w_share(0)
-    w_sum(0)
-    done = {seq[0]}
-    arrive = sorted(range(1, Z), key=lambda k: (bin(k).count("1"), k))
-    for kz in arrive:
-        forward(kz)
-        nxt = [k for k in seq if k not in done]
-        if nxt:
-            lat_share(nxt[0])
-            done.add(nxt[0])
-    for kz in seq:
-        if kz not in done:
-            lat_share(kz)
-    for kz in order[1:]:
-        w_share(kz)
-        w_sum(kz)
-    for kz in order[1:]:
+    lat_next()
+    w_sum(0, 0)
+    for kx in xs:
+        w_share(0, kx)
+    lat_next()
+    for kx in xs:
+        w_sum(0, kx)
+    once = [k for k in tail if k & (k - 1) == 0]
+    twice = [k for k in tail if k & (k - 1)]
+    for group in (once, twice):
+        for kz in group:
+            forward(kz)
+        for kz in group:
+            w_share(kz, 0)
+        for kz in group:
+            w_sum(kz, 0)
+    lat_next()
+    lat_sum_x(tail[0])
+    for kz in once:
+        for kx in xs:
+            w_share(kz, kx)
+            w_sum(kz, kx)
+    lat_next()
+    for kz in twice:
+        for kx in xs:
+            w_share(kz, kx)
+            w_sum(kz, kx)
+    for kz in tail[1:]:
         lat_sum_x(kz)
     queries()
     lat_sum_x(0)
 
-    @pl.loop(0, NC)
-    def _(c):
-        mine = y * CORES + core
-        send_ws(mine, c).wait_recv()
-        total = part[mine, c].astype(f32) + sib[y, c].astype(f32)
-        for k in range(1, Y):
-            p = lax.rem(y + k, Y)
-            other = pltpu.make_async_remote_copy(
-                src_ref=part.at[p * CORES + core, c], dst_ref=ybuf.at[k - 1, c],
-                send_sem=wy_s.at[k - 1, c], recv_sem=wy_r.at[k - 1, c],
-                device_id=(p * CORES + core, head), device_id_type=MESH)
-            other.wait_recv()
-            total = total + ybuf[k - 1, c].astype(f32)
-        grad_ref[:, pl.ds(pl.multiple_of(c * C, C), C)] = total
+    for j in range(Q):
+        @pl.loop(0, NC)
+        def _(c):
+            mine = (y * CORES + core) * Q + j
+            send_ws(mine, c).wait_recv()
+            total = part[mine, c].astype(f32) + sib[y, j, c].astype(f32)
+            for k in range(1, Y):
+                copy_wy(mine, lax.rem(y + k, Y), k - 1, c).wait_recv()
+                total = total + ybuf[k - 1, j, c].astype(f32)
+            grad_ref[j * B:(j + 1) * B, pl.ds(pl.multiple_of(c * C, C), C)] = total
 
     for kz in range(Z):
         for bit in low(kz):
@@ -266,10 +277,12 @@
 
     @pl.loop(0, NC)
     def _(c):
-        for p in range(Y):
-            send_ws(p * CORES + 1 - core, c).wait_send()
-        for k in range(1, Y):
-            send_wy(lax.rem(y - k + Y, Y), c).wait_send()
+        for j in range(Q):
+            for p in range(Y):
+                send_ws((p * CORES + 1 - core) * Q + j, c).wait_send()
+            for k in range(1, Y):
+                p = lax.rem(y - k + Y, Y)
+                copy_wy((p * CORES + core) * Q + j, p, k - 1, c).wait_send()
         for t in range(NQ):
             q_out(t, c).wait()
 
@@ -280,7 +293,7 @@
     X = 1 << (int(math.log2(n_head)) // 2)
     Z = n_head // X
     Y = n_dp // CORES
-    R = n_dp // Z
+    Q = n_head // n_dp
     rows = D // n_dp
     C = 1024 if width % 1024 == 0 else 512
     NC = width // C
@@ -293,7 +306,7 @@
     vmem = pl.BlockSpec(memory_space=pltpu.VMEM)
     hbm = pl.BlockSpec(memory_space=pl.ANY)
     queries, lgt, grad = pl.pallas_call(
-        functools.partial(kernel, (Z, X, Y, R, NC, C, NT, T, NQ, TQ)),
+        functools.partial(kernel, (Z, X, Y, Q, NC, C, NT, T, NQ, TQ)),
         out_shape=(
             jax.ShapeDtypeStruct((T_all, width), bf),
             jax.ShapeDtypeStruct((B, T_all), bf),
@@ -305,9 +318,9 @@
             pltpu.VMEM((Z, X * B, width), bf),
             pltpu.VMEM((T_all, width), bf),
             pltpu.VMEM((Z, X, B, T_all), bf),
-            pltpu.VMEM((n_dp, NC, rows, C), bf),
-            pltpu.VMEM((Y, NC, rows, C), bf),
-            pltpu.VMEM((max(Y - 1, 1), NC, rows, C), bf),
+            pltpu.VMEM((n_head, NC, B, C), bf),
+            pltpu.VMEM((Y, Q, NC, B, C), bf),
+            pltpu.VMEM((max(Y - 1, 1), Q, NC, B, C), bf),
             pltpu.VMEM((Z, X, B, T_all), bf),
             pltpu.VMEM((X - 1, Z, B, T_all), bf),
             pltpu.VMEM((Z - 1, B, T_all), bf),
@@ -316,7 +329,7 @@
             sem((Z,)), sem, sem, sem((NQ, NC)),
             sem((Z,)), sem((Z,)), sem((Z, X)), sem((Z, X)),
             sem((Z, X)), sem((Z, X)), sem((Z,)), sem((Z,)),
-            sem((Y, NC)), sem((Y, NC)), sem((max(Y - 1, 1), NC)), sem((max(Y - 1, 1), NC)),
+            sem((Y, Q, NC)), sem((Y, Q, NC)), sem((max(Y - 1, 1), Q, NC)), sem((max(Y - 1, 1), Q, NC)),
         ],
         compiler_params=pltpu.CompilerParams(
             collective_id=0, has_side_effects=True, vmem_limit_bytes=60 * 1024 * 1024

time: 126 us -> 104 us (0.83)
  Pallas kernels: 110 us -> 86.8 us
    pallas_call x1, Pallas kernels: 110 us -> 86.8 us  [on_device(): pl.pallas_call(functools.partial(kernel, (Z, X, Y, Q, NC, C, NT, T, NQ, T...]
where the time goes in v2:
time: 104 us
  Pallas kernels  86.8 us (83%)
  other arithmetic  12.6 us (12%)
  local copies, waits for them, and re-layouts  3.46 us (3%)
    pallas_call x1, Pallas kernels, on_device(): pl.pallas_call(functools.partial(kernel, (Z, X, Y, Q, NC, C, NT, T, NQ, T...  86.8 us
    sub x1, other arithmetic, on_device(): master - 0.01 * (first_hat / (jnp.sqrt(second_hat) + 1e-08) + 0.1 * master)  12.6 us
    unnamed x6, local copies, waits for them, and re-layouts  3.46 us

profile of v2, /device:TPU:12, one launch (start us, length us, event | category | flops | bytes accessed | tf_op | source)
XLA Modules:
  0.0 103.5 jit_solution(10027212540690496391)
XLA Ops:
  0.6 86.8 %shard_map.101 = (bf16[1024,3072]{1,0:T(8,128)(2,1)}, bf16[192,1024]{1,0:T(8,128)(2,1)}, f32[384,3072]{1,0:T(8,128)}) custom-call(bf16[192,1024]{1,0:T(8,128)(2,1)} %bitcast.3, bf16[1536,3072]{1,0:T(8,128)(2,1)} %w_hbm.1, bf16[1024,3072]{1,0:T(8,128)(2,1)} %qg_hbm.1), custom_call_target="tpu_custom_call" | custom-call | flops 28991029248 | bytes 31457280 | tf_op jit(solution)/shard_map/pallas_call | solution.py:308
  87.4 0.0 copy-start
  87.4 12.6 %multiply_subtract_fusion = (f32[384,3072]{1,0:T(8,128)}, f32[384,3072]{1,0:T(8,128)}, f32[384,3072]{1,0:T(8,128)}) fusion(f32[384,3072]{1,0:T(8,128)} %param.9, f32[384,3072]{1,0:T(8,128)} %get-tuple-element.10, f32[384,3072]{1,0:T(8,128)} %param.10, f32[384,3072]{1,0:T(8,128)} %param.11), kind=kLoop, calls=%fused_computation.2 | loop fusion | flops 17694720 | bytes 33030144 | tf_op jit(solution)/shard_map/sub | solution.py:346
  100.1 0.0 copy-done
  100.1 0.0 copy-start.1
  100.1 2.7 %copy.13 = bf16[1024,3072]{1,0:T(8,128)(2,1)} copy(bf16[1024,3072]{1,0:T(8,128)(2,1)S(1)} %copy-done) | data formatting | bytes 12582912
  102.8 0.0 copy-done.1
  102.8 0.7 copy.14
Async XLA Ops:
  87.4 12.6 %copy-start = (bf16[1024,3072]{1,0:T(8,128)(2,1)S(1)}, bf16[1024,3072]{1,0:T(8,128)(2,1)}, u32[]{:S(2)}) copy-start(bf16[1024,3072]{1,0:T(8,128)(2,1)} %get-tuple-element.19) | copy-start | bytes 18874372
  100.1 2.7 %copy-start.1 = (bf16[192,1024]{1,0:T(8,128)(2,1)S(1)}, bf16[192,1024]{1,0:T(8,128)(2,1)}, u32[]{:S(2)}) copy-start(bf16[192,1024]{1,0:T(8,128)(2,1)} %get-tuple-element.9) | copy-start | bytes 1179652
